TPU v7x, 512 devices: a whole 4x8x8 slice. The times are simulated.
512 devices in a mesh: row: 32 (over y, x), col: 16 (over z, core).
Axes of the slice: x: 4, y: 8, z: 8, core: 2. Of those that a mesh axis runs over, the one named last changes fastest.
Arguments:
- tiles: float32 [32, 16, 2, 256, 256], P('row', 'col'), may hold values from -0.375 to 0.375
- tile_rows: int32 [32, 16, 2], P('row', 'col'), may hold values from 0 to 7
- tile_cols: int32 [32, 16, 2], P('row', 'col'), may hold values from 0 to 15, as said below
- tile_counts: int32 [32, 16], P('row', 'col'), may hold values from 1 to 2, as said below
- diagonal: float32 [65536], P(('row', 'col')), may hold values from 0.5 to 4
- basis: float32 [16, 16, 65536], P(None, None, ('row', 'col')), may hold values from -6 to 6
- start: float32 [16, 65536], P(None, ('row', 'col')), may hold values from -8 to 8
Outputs:
- blocks: float32 [2, 16, 65536], P(None, None, ('row', 'col'))
- factors: float32 [2, 16, 16], replicated
Inputs may be any that keep to these rules, and one draw needn't show every extreme that they name: `tile_cols`: the slots of one device name distinct tile-column blocks. `tile_counts`: slots from this count on are padding.
All inputs are finite; a program needn't handle non-finite values.
Results may differ from a plain program's by a relative error of at most 0.004.
Values may be sent and summed in bfloat16 or wider, within the bound.
A program may use at most 64 MiB of HBM per device.

v0:
```python
import jax
import jax.numpy as jnp
from jax import lax
from jax.sharding import PartitionSpec as P

TILE = 256


PRECISE = lax.Precision.HIGHEST


def broadcast(value, axis, source):
    kept = jnp.where(lax.axis_index(axis) == source, value, 0).astype(value.dtype)
    return lax.psum(kept, axis)


def project(stack_all, field, inv_total):
    return jnp.einsum("mkn,ln->mkl", stack_all, field, precision=PRECISE) * inv_total


def remove(field, coeffs, stack_all):
    return field - jnp.einsum("mkl,mkn->ln", coeffs, stack_all, precision=PRECISE)


def local(tiles, tile_rows, tile_cols, tile_counts, diagonal, basis, start):
    vec_width, share_rows = start.shape
    col_count = lax.axis_size("col")
    row_count = lax.axis_size("row")
    inv_total = 1.0 / (share_rows * col_count * row_count)
    row_id = lax.axis_index("row")
    col_id = lax.axis_index("col")
    plates = tiles[0, 0]
    local_rows = tile_rows[0, 0]
    local_cols = tile_cols[0, 0]
    filled = tile_counts[0, 0]
    slot_count = plates.shape[0]
    group_rows = share_rows * col_count
    blocks = group_rows // TILE
    row_block = row_id * blocks + local_rows
    col_block = (col_id + col_count * (local_cols // blocks)) * blocks + local_cols % blocks
    is_live = jnp.arange(slot_count, dtype=jnp.int32) < filled
    factor = jnp.where(is_live, jnp.where(row_block == col_block, 0.5, 1.0), 0.0).astype(
        jnp.float32
    )
    row_pick = (local_rows[:, None] == jnp.arange(blocks)[None, :]).astype(jnp.float32) * factor[
        :, None
    ]
    col_pick = (local_cols[:, None] == jnp.arange(2 * blocks)[None, :]).astype(
        jnp.float32
    ) * factor[:, None]
    half_id = row_id // col_count
    stack_all = jnp.concatenate([basis, start[None]], axis=0)
    current = start
    outputs = []
    lowers = []
    for step_index in range(2):
        gathered = lax.all_gather(current, "col", axis=1, tiled=True)
        halves = []
        for half_index in range(2):
            halves.append(
                broadcast(
                    gathered.astype(jnp.bfloat16), "row", col_id + half_index * col_count
                ).astype(gathered.dtype)
            )
        columns = jnp.concatenate(halves, axis=1).reshape(vec_width, 2 * blocks, TILE)
        rowwise = gathered.reshape(vec_width, blocks, TILE)
        from_cols = columns[:, local_cols, :]
        from_rows = rowwise[:, local_rows, :]
        row_terms = jnp.einsum("ksj,sij->ksi", from_cols, plates, precision=PRECISE)
        col_terms = jnp.einsum("ksi,sij->ksj", from_rows, plates, precision=PRECISE)
        row_part = jnp.einsum("ksi,sa->kai", row_terms, row_pick, precision=PRECISE).reshape(
            vec_width, group_rows
        )
        col_part = jnp.einsum("ksj,sb->kbj", col_terms, col_pick, precision=PRECISE).reshape(
            vec_width, 2 * group_rows
        )
        totals = lax.psum(row_part.astype(jnp.bfloat16), "col").astype(jnp.float32)
        own_rows = lax.dynamic_slice_in_dim(totals, col_id * share_rows, share_rows, 1)
        column_sums = lax.psum(col_part.astype(jnp.bfloat16), "row").astype(jnp.float32)
        own_half = lax.dynamic_slice_in_dim(column_sums, half_id * group_rows, group_rows, 1)
        spread = broadcast(own_half.astype(jnp.bfloat16), "col", row_id % col_count).astype(
            own_half.dtype
        )
        own_cols = lax.dynamic_slice_in_dim(spread, col_id * share_rows, share_rows, 1)
        image_block = own_rows + own_cols + diagonal[None, :] * current
        first_proj = lax.psum(project(stack_all, image_block, inv_total), ("row", "col"))
        once_done = remove(image_block, first_proj, stack_all)
        second_proj = lax.psum(project(stack_all, once_done, inv_total), ("row", "col"))
        twice_done = remove(once_done, second_proj, stack_all)
        gram_block = lax.psum(
            jnp.dot(twice_done, twice_done.T, precision=PRECISE) * inv_total, ("row", "col")
        )
        lower_factor = jnp.linalg.cholesky(gram_block)
        fresh_block = lax.linalg.triangular_solve(
            lower_factor, twice_done, left_side=True, lower=True
        )
        outputs.append(fresh_block)
        lowers.append(lower_factor)
        stack_all = jnp.concatenate([stack_all, fresh_block[None]], axis=0)
        current = fresh_block
    return (jnp.stack(outputs), jnp.stack(lowers))


def solution(mesh):
    placed = (
        P("row", "col", None, None, None),
        P("row", "col", None),
        P("row", "col", None),
        P("row", "col"),
        P(("row", "col")),
        P(None, None, ("row", "col")),
        P(None, ("row", "col")),
    )
    return jax.shard_map(
        local,
        mesh=mesh,
        in_specs=placed,
        out_specs=(P(None, None, ("row", "col")), P()),
        check_vma=False,
    )
```

profile of v0, /device:TPU:1, one launch (start us, length us, event | category | flops | bytes accessed | tf_op | source)
XLA Modules:
  0.0 1191.2 jit_solution(17586831793094694362)
XLA Ops:
  7.2 0.0 all-reduce.11.cloned.1.call-start
  8.0 24.8 %all_gather.6 = f32[16,2048]{1,0:T(8,128)S(1)} all-gather(f32[16,128]{1,0:T(8,128)S(1)} %copy-done.1), channel_id=1, replica_groups=mesh['row'=32,'col'=16] {'col'}, dimensions={1}, use_global_device_ids=true | all-gather | bytes 139264 | tf_op jit(solution)/shard_map/all_gather | solution.py:57
  32.9 0.6 gather_fusion
  33.4 0.4 fusion.8
  33.8 0.7 copy-done.7
  34.5 0.5 convolution_convert_fusion.1
  35.0 0.7 copy.38
  35.7 0.7 broadcast_select_fusion.3
  36.4 0.0 all-reduce.15.cloned.1.call-start
  36.5 147.7 %all-reduce.11.cloned.1.call-done = (bf16[16,4096]{1,0:T(8,128)(2,1)}, bf16[16,2048]{1,0:T(8,128)(2,1)}, bf16[16,2048]{1,0:T(8,128)(2,1)}) async-done(((bf16[16,4096]{1,0:T(8,128)(2,1)}, bf16[16,2048]{1,0:T(8,128)(2,1)}, bf16[16,2048]{1,0:T(8,128)(2,1)}), (bf16[16,4096]{1,0:T(8,128)(2,1)}, bf16[16,2048]{1,0:T(8,128)(2,1)}, bf16[16,2048]{1,0:T(8,128)(2,1)})) %all-reduce.11.cloned.1.call-update) | async-done | bytes 262160 | tf_op jit(solution)/shard_map/psum | solution.py:79
  184.2 0.9 pad_maximum_fusion.6
  185.1 0.5 gather_fusion.2
  185.7 0.3 fusion.10
  186.1 0.4 convolution_convert_fusion.3
  186.4 0.6 copy.37
  187.1 0.6 fusion.12
  187.7 0.0 all-reduce.9.cloned.1.call-start
  187.8 0.2 copy-done.2
  188.1 115.6 %all-reduce.15.cloned.1.call-done = (bf16[16,2048]{1,0:T(8,128)(2,1)}, bf16[16,2048]{1,0:T(8,128)(2,1)}) async-done(((bf16[16,2048]{1,0:T(8,128)(2,1)}, bf16[16,2048]{1,0:T(8,128)(2,1)}), (bf16[16,2048]{1,0:T(8,128)(2,1)}, bf16[16,2048]{1,0:T(8,128)(2,1)})) %all-reduce.15.cloned.1.call-update) | async-done | bytes 131088 | tf_op jit(solution)/shard_map/psum | solution.py:14
  303.7 0.7 copy-done.6
  304.3 1.8 convolution_multiply_fusion.3
  306.1 99.0 %psum.117 = f32[17,16,16]{0,2,1:T(8,128)S(1)} all-reduce(f32[17,16,16]{0,2,1:T(8,128)S(1)} %convolution_multiply_fusion.3), channel_id=1, replica_groups=mesh['row'=32,'col'=16] {'row','col'}, use_global_device_ids=true, to_apply=%region_5.6 | all-reduce | flops 4352 | bytes 34816 | tf_op jit(solution)/shard_map/psum | solution.py:86
  405.1 1.1 fusion
  406.2 1.1 convolution_multiply_fusion.2
  407.3 93.7 %psum.118 = f32[17,16,16]{0,2,1:T(8,128)S(1)} all-reduce(f32[17,16,16]{0,2,1:T(8,128)S(1)} %convolution_multiply_fusion.2), channel_id=1, replica_groups=mesh['row'=32,'col'=16] {'row','col'}, use_global_device_ids=true, to_apply=%region_6.7 | all-reduce | flops 4352 | bytes 34816 | tf_op jit(solution)/shard_map/psum | solution.py:88
  501.0 0.4 fusion.1
  501.4 0.1 convolution_multiply_fusion.5
  501.6 95.3 %psum.119 = f32[16,16]{0,1:T(8,128)S(1)} all-reduce(f32[16,16]{0,1:T(8,128)S(1)} %convolution_multiply_fusion.5), channel_id=1, replica_groups=mesh['row'=32,'col'=16] {'row','col'}, use_global_device_ids=true, to_apply=%region_7.8 | all-reduce | flops 256 | bytes 2048 | tf_op jit(solution)/shard_map/psum | solution.py:90
  596.9 0.1 copy.20
  596.9 1.5 cholesky.44
  598.4 0.6 compare_reduce_fusion.1
  599.1 0.6 fusion.36
  599.7 1.2 custom-call.6
  601.0 0.2 fusion.30
  601.2 17.6 %all_gather.7 = f32[16,2048]{1,0:T(8,128)S(1)} all-gather(f32[16,128]{1,0:T(8,128)S(1)} %fusion.30), channel_id=1, replica_groups=mesh['row'=32,'col'=16] {'col'}, dimensions={1}, use_global_device_ids=true | all-gather | bytes 139264 | tf_op jit(solution)/shard_map/all_gather | solution.py:57
  618.7 0.7 broadcast_select_fusion.2
  619.4 0.6 gather_fusion.1
  620.0 0.4 fusion.4
  620.3 0.5 convolution_convert_fusion
  620.9 0.7 copy.40
  621.6 0.0 all-reduce.13.cloned.1.call-start
  621.7 145.5 %all-reduce.9.cloned.1.call-done = (bf16[16,4096]{1,0:T(8,128)(2,1)}, bf16[16,2048]{1,0:T(8,128)(2,1)}, bf16[16,2048]{1,0:T(8,128)(2,1)}) async-done(((bf16[16,4096]{1,0:T(8,128)(2,1)}, bf16[16,2048]{1,0:T(8,128)(2,1)}, bf16[16,2048]{1,0:T(8,128)(2,1)}), (bf16[16,4096]{1,0:T(8,128)(2,1)}, bf16[16,2048]{1,0:T(8,128)(2,1)}, bf16[16,2048]{1,0:T(8,128)(2,1)})) %all-reduce.9.cloned.1.call-update) | async-done | bytes 262160 | tf_op jit(solution)/shard_map/psum | solution.py:79
  767.2 1.5 fusion.13
  768.7 0.5 gather_fusion.3
  769.3 0.3 fusion.6
  769.6 0.4 convolution_convert_fusion.2
  770.0 0.6 copy.39
  770.7 115.9 %all-reduce.13.cloned.1.call-done = (bf16[16,2048]{1,0:T(8,128)(2,1)}, bf16[16,2048]{1,0:T(8,128)(2,1)}) async-done(((bf16[16,2048]{1,0:T(8,128)(2,1)}, bf16[16,2048]{1,0:T(8,128)(2,1)}), (bf16[16,2048]{1,0:T(8,128)(2,1)}, bf16[16,2048]{1,0:T(8,128)(2,1)})) %all-reduce.13.cloned.1.call-update) | async-done | bytes 131088 | tf_op jit(solution)/shard_map/psum | solution.py:14
  886.6 1.8 convolution_multiply_fusion.1
  888.4 99.0 %psum.125 = f32[18,16,16]{0,2,1:T(8,128)S(1)} all-reduce(f32[18,16,16]{0,2,1:T(8,128)S(1)} %convolution_multiply_fusion.1), channel_id=1, replica_groups=mesh['row'=32,'col'=16] {'row','col'}, use_global_device_ids=true, to_apply=%region_15.18 | all-reduce | flops 4608 | bytes 36864 | tf_op jit(solution)/shard_map/psum | solution.py:86
  987.4 1.1 fusion.2
  988.5 1.1 convolution_multiply_fusion
  989.6 93.7 %psum.126 = f32[18,16,16]{0,2,1:T(8,128)S(1)} all-reduce(f32[18,16,16]{0,2,1:T(8,128)S(1)} %convolution_multiply_fusion), channel_id=1, replica_groups=mesh['row'=32,'col'=16] {'row','col'}, use_global_device_ids=true, to_apply=%region_16.19 | all-reduce | flops 4608 | bytes 36864 | tf_op jit(solution)/shard_map/psum | solution.py:88
  1083.3 0.4 fusion.3
  1083.7 0.1 convolution_multiply_fusion.4
  1083.9 95.3 %psum.127 = f32[16,16]{0,1:T(8,128)S(1)} all-reduce(f32[16,16]{0,1:T(8,128)S(1)} %convolution_multiply_fusion.4), channel_id=1, replica_groups=mesh['row'=32,'col'=16] {'row','col'}, use_global_device_ids=true, to_apply=%region_17.20 | all-reduce | flops 256 | bytes 2048 | tf_op jit(solution)/shard_map/psum | solution.py:90
  1179.2 0.1 copy.26
  1179.2 1.5 cholesky.55
  1180.7 0.6 compare_reduce_fusion
  1181.4 0.6 fusion.37
  1182.0 1.2 custom-call.7
  1183.2 0.2 convolution_bitcast_fusion
  1183.5 0.6 pad_maximum_fusion.13
  1184.1 0.6 pad_maximum_fusion.12
  (34 shorter events, 0.3 us)
Async XLA Ops:
  7.2 26.3 %copy-start = (f32[1,1,2,256,256]{4,3,2,1,0:T(8,128)S(1)}, f32[1,1,2,256,256]{4,3,2,1,0:T(8,128)}, u32[]{:S(2)}) copy-start(f32[1,1,2,256,256]{4,3,2,1,0:T(8,128)} %param.10) | copy-start | bytes 1572868
  7.2 177.1 %all-reduce.11.cloned.1.call-start = ((), (), s32[]{:S(2)}) async-start(), calls=%async_computation.1 | async-start | bytes 524288 | tf_op jit(solution)/shard_map/psum | solution.py:79
  7.2 0.8 copy-start.1
  7.2 0.7 copy-start.8
  33.8 0.7 copy-start.7
  36.4 267.2 %all-reduce.15.cloned.1.call-start = ((), (), s32[]{:S(2)}) async-start(), calls=%async_computation.3 | async-start | bytes 262144 | tf_op jit(solution)/shard_map/psum | solution.py:14
  186.0 1.0 copy-start.5
  187.1 0.9 copy-start.2
  187.7 579.4 %all-reduce.9.cloned.1.call-start = ((), (), s32[]{:S(2)}) async-start(), calls=%async_computation | async-start | bytes 524288 | tf_op jit(solution)/shard_map/psum | solution.py:79
  303.7 0.7 copy-start.6
  621.6 265.0 %all-reduce.13.cloned.1.call-start = ((), (), s32[]{:S(2)}) async-start(), calls=%async_computation.2 | async-start | bytes 262144 | tf_op jit(solution)/shard_map/psum | solution.py:14
  767.2 1.5 copy-start.3
  767.2 1.5 copy-start.4
Sparse Core Ops, SparseCore 0:
  36.5 147.6 all-reduce.10
  187.9 115.7 all-reduce.14
  621.7 145.3 all-reduce.8
  770.8 115.7 all-reduce.12
where the time goes:
time: 1190 us
  blocking collectives  618 us (52%)
  waiting for transfers between devices  525 us (44%)
  between operations  14.7 us (1%)
  other arithmetic  13.6 us (1%)
  matrix products  12.8 us (1%)
    psum x2, waiting for transfers between devices, local(): lax.psum(col_part.astype(jnp.bfloat16), 'row').astype(jnp.float32)  293 us
    psum x2, waiting for transfers between devices, broadcast(): return lax.psum(kept, axis)  232 us
    psum x2, blocking collectives, local(): lax.psum(project(stack_all, image_block, inv_total), ('row', 'col'))  198 us
    psum x2, blocking collectives, local(): lax.psum(jnp.dot(twice_done, twice_done.T, precision=PRECISE) * inv_total...  191 us
    psum x2, blocking collectives, local(): lax.psum(project(stack_all, once_done, inv_total), ('row', 'col'))  187 us
    all_gather x2, blocking collectives, local(): gathered = lax.all_gather(current, 'col', axis=1, tiled=True)  42.4 us
  transfers between devices with their start and end apart: 4, of which 4 were waited for; matrix products, arithmetic and copies ran while one was open for 0% of the time, Pallas kernels for 0%

commit v1 on v0

v1 whole, which is shorter than its diff:
```python
import functools

import jax
import jax.numpy as jnp
from jax import lax
from jax.experimental import pallas as pl
from jax.experimental.pallas import tpu as pltpu
from jax.sharding import PartitionSpec as P

MESH = pl.DeviceIdType.MESH
F32, BF16 = jnp.float32, jnp.bfloat16
HIGH = lax.Precision.HIGHEST
ROWS, COLS, YS, XS = 32, 16, 8, 4
BW, LANES, TILE = 16, 128, 256
KNOWN, FRESH, IMAGE, DEPTH = 272, 272, 288, 384


def dot(a, b, precision=HIGH):
    return lax.dot_general(a, b, (((1,), (0,)), ((), ())), precision=precision, preferred_element_type=F32)


def dot_t(a, b, precision=HIGH):
    return lax.dot_general(a, b, (((1,), (1,)), ((), ())), precision=precision, preferred_element_type=F32)


def at(row, col):
    return {"row": row, "col": col}


def push(src, dst, send_sem, recv_sem, target):
    pltpu.make_async_remote_copy(
        src_ref=src, dst_ref=dst, send_sem=send_sem, recv_sem=recv_sem, device_id=target, device_id_type=MESH
    ).start()


def drain(ref, sem):
    pltpu.make_async_copy(ref, ref, sem).wait()


def loop(low, high, body):
    def run(k, carry):
        body(k)
        return carry

    lax.fori_loop(low, high, run, 0)


def factor(gram):
    row = lax.broadcasted_iota(jnp.int32, (BW, LANES), 0)
    lane = lax.broadcasted_iota(jnp.int32, (BW, LANES), 1)
    eye = (lane == row + BW).astype(F32)
    work = jnp.concatenate([gram, jnp.zeros((BW, LANES - BW), F32)], axis=1) + eye
    lower = jnp.zeros((BW, LANES), F32)
    scale = jnp.zeros((BW, LANES), F32)
    for j in range(BW):
        pivot_row = work[j : j + 1, :]
        column = work[:, j : j + 1]
        pivot = pivot_row[:, j : j + 1]
        root = 1.0 / jnp.sqrt(pivot)
        lower = jnp.where((lane == j) & (row >= j), column * root, lower)
        scale = jnp.where(row == j, root, scale)
        step = jnp.where(row > j, column * (1.0 / pivot), 0.0)
        work = work - step * pivot_row
    inverse = (work * scale)[:, BW : 2 * BW]
    return lower[:, :BW], inverse


def kernel(
    tiles_ref, rows_ref, cols_ref, count_ref, diag_ref, basis_ref, start_ref,
    blocks_ref, factors_ref,
    stack, plates, split, dg, sent, vrow, vcol, prow, pcol, grow, gcol,
    c_part, c_col, c_sum, c_row, c_all, c_got,
    m_part, m_col, m_y, m_x, m_one, m_two, m_all, m_got, gram, clean,
    load_sem, v_send, vrow_sem, vcol_sem, p_send, grow_sem, gcol_sem, ar_send, ar_sem, m_send, m_sem,
):
    r, c = lax.axis_index("row"), lax.axis_index("col")
    y, x = r // XS, lax.rem(r, XS)
    twin = lax.rem(r, COLS)
    own = c == twin
    inv_total = 1.0 / (ROWS * COLS * LANES)

    loads = [
        pltpu.make_async_copy(basis_ref, stack.at[pl.ds(0, 256)], load_sem.at[0]),
        pltpu.make_async_copy(start_ref, stack.at[pl.ds(256, BW)], load_sem.at[1]),
        pltpu.make_async_copy(tiles_ref, plates, load_sem.at[2]),
        pltpu.make_async_copy(diag_ref, dg, load_sem.at[3]),
    ]
    for each in loads:
        each.start()

    barrier = pltpu.get_barrier_semaphore()

    def greet(target):
        pl.semaphore_signal(barrier, inc=1, device_id=target, device_id_type=MESH)

    def greet_rows(k):
        greet(at(lax.rem(r + k, ROWS), c))

    def greet_cols(k):
        greet(at(r, lax.rem(c + k, COLS)))

    def greet_twins(k):
        greet(at(lax.rem(r + k, ROWS), twin))
        greet(at(c + COLS * (k // COLS), lax.rem(k, COLS)))

    loop(0, ROWS, greet_twins)
    loop(1, ROWS, greet_rows)
    loop(1, COLS, greet_cols)

    stack[FRESH:DEPTH, :] = jnp.zeros((DEPTH - FRESH, LANES), F32)
    loads[0].wait()
    loads[1].wait()
    low, mid, last = stack[0:128, :], stack[128:256, :], stack[256:DEPTH, :][:BW]
    sent[0] = last.astype(BF16)
    m_part[:, 0] = dot_t(low, low).reshape(COLS, 8, LANES)
    m_part[:, 1] = dot_t(low, mid).reshape(COLS, 8, LANES)
    m_part[:, 2] = dot_t(mid, mid).reshape(COLS, 8, LANES)
    edge = dot_t(last, stack[...])
    m_part[:, 3] = jnp.zeros((COLS, 8, LANES), F32)
    for k in range(COLS):
        for j in range(3):
            m_part[k, 3, j : j + 1, :] = edge[k : k + 1, LANES * j : LANES * (j + 1)]
    m_col[c] = m_part[c]
    loads[2].wait()
    loads[3].wait()
    for s in range(2):
        whole = plates[s]
        high = whole.astype(BF16)
        split[s, 0] = high
        split[s, 1] = (whole - high.astype(F32)).astype(BF16)

    weights = []
    for s in range(2):
        row_block = r * 8 + rows_ref[s]
        half = cols_ref[s] // 8
        col_block = (c + COLS * half) * 8 + (cols_ref[s] - 8 * half)
        live = jnp.where(row_block == col_block, 0.5, 1.0)
        weights.append(jnp.where(s < count_ref[0], live, 0.0).astype(F32))

    pl.semaphore_wait(barrier, 15 + 31 + 64)

    def send_vectors(k):
        src = sent.at[k]
        slot = COLS * (r // COLS) + c

        def to_twin(n):
            target = lax.rem(r + n, ROWS)
            push(src, vcol.at[k, slot], v_send.at[k], vcol_sem.at[k, r // COLS], at(target, twin))

        loop(1, ROWS, to_twin)

        @pl.when(own)
        def _():
            vcol[k, slot] = sent[k]

        @pl.when(jnp.logical_not(own))
        def _():
            to_twin(0)

        def to_col(n):
            push(src, vrow.at[k, c], v_send.at[k], vrow_sem.at[k], at(r, lax.rem(c + n, COLS)))

        loop(1, COLS, to_col)
        vrow[k, c] = sent[k]

    def drain_sized(ref, k, full, cond, sem):
        @pl.when(cond)
        def _():
            drain(ref.at[k, pl.ds(0, full - 1)], sem)

        @pl.when(jnp.logical_not(cond))
        def _():
            drain(ref.at[k, pl.ds(0, full)], sem)

    def products(k, inverse):
        drain(vrow.at[k, pl.ds(0, COLS - 1)], vrow_sem.at[k])
        terms = []
        for s in range(2):
            b = 2 * rows_ref[s]
            vec = jnp.concatenate([vrow[k, b], vrow[k, b + 1]], axis=1)
            term = dot(vec, split[s, 0], None) + dot(vec, split[s, 1], None)
            terms.append(term if inverse is None else dot(inverse, term))
        for b in range(2 * 8):
            part = sum(terms[s] * jnp.where(cols_ref[s] == b, weights[s], 0.0) for s in range(2)).astype(BF16)
            pcol[k, 2 * b] = part[:, :LANES]
            pcol[k, 2 * b + 1] = part[:, LANES:]

        def to_col_owner(n):
            n16 = lax.rem(c + n, COLS)
            for h in range(2):
                push(pcol.at[k, COLS * h + n16], gcol.at[k, r], p_send.at[k], gcol_sem.at[k], at(c + COLS * h, n16))

        loop(1, COLS, to_col_owner)
        for h in range(2):
            mine = r == c + COLS * h

            @pl.when(mine)
            def _():
                gcol[k, r] = pcol[k, COLS * h + c]

            @pl.when(jnp.logical_not(mine))
            def _():
                push(pcol.at[k, COLS * h + c], gcol.at[k, r], p_send.at[k], gcol_sem.at[k], at(c + COLS * h, c))

        for h in range(2):

            @pl.when(r == c + COLS * h)
            def _():
                drain(vcol.at[k, pl.ds(0, COLS - 1)], vcol_sem.at[k, h])

            @pl.when(r != c + COLS * h)
            def _():
                drain(vcol.at[k, pl.ds(0, COLS)], vcol_sem.at[k, h])

        terms = []
        for s in range(2):
            b = 2 * cols_ref[s]
            vec = jnp.concatenate([vcol[k, b], vcol[k, b + 1]], axis=1)
            term = dot_t(vec, split[s, 0], None) + dot_t(vec, split[s, 1], None)
            terms.append(term if inverse is None else dot(inverse, term))
        for b in range(8):
            part = sum(terms[s] * jnp.where(rows_ref[s] == b, weights[s], 0.0) for s in range(2)).astype(BF16)
            prow[k, 2 * b] = part[:, :LANES]
            prow[k, 2 * b + 1] = part[:, LANES:]

        def to_row_owner(n):
            n16 = lax.rem(c + n, COLS)
            push(prow.at[k, n16], grow.at[k, c], p_send.at[k], grow_sem.at[k], at(r, n16))

        loop(1, COLS, to_row_owner)
        grow[k, c] = prow[k, c]

    def image(k, current):
        drain_sized(gcol, k, ROWS, own, gcol_sem.at[k])
        drain(grow.at[k, pl.ds(0, COLS - 1)], grow_sem.at[k])
        total = dg[...] * current
        total += jnp.sum(gcol[k].astype(F32), axis=0)
        total += jnp.sum(grow[k].astype(F32), axis=0)
        return total

    def inner_send(k, w):
        stack[IMAGE : IMAGE + BW, :] = w
        partial = dot_t(w, stack[...])
        for n in range(BW):
            c_part[k, n] = partial[n : n + 1, :]

        def to_col(n):
            n16 = lax.rem(c + n, COLS)
            push(c_part.at[k, n16], c_col.at[k, c], ar_send.at[k, 0], ar_sem.at[k, 0], at(r, n16))

        loop(1, COLS, to_col)
        c_col[k, c] = c_part[k, c]

    def inner_rows(k):
        drain(c_col.at[k, pl.ds(0, COLS - 1)], ar_sem.at[k, 0])
        c_sum[k] = jnp.sum(c_col[k], axis=0)

        def to_row(n):
            push(c_sum.at[k], c_row.at[k, r], ar_send.at[k, 1], ar_sem.at[k, 1], at(lax.rem(r + n, ROWS), c))

        loop(1, ROWS, to_row)
        c_row[k, r] = c_sum[k]

    def inner_cols(k):
        drain(c_row.at[k, pl.ds(0, ROWS - 1)], ar_sem.at[k, 1])
        c_all[k] = jnp.sum(c_row[k], axis=0) * inv_total

        def to_col(n):
            push(c_all.at[k], c_got.at[k, c], ar_send.at[k, 2], ar_sem.at[k, 2], at(r, lax.rem(c + n, COLS)))

        loop(1, COLS, to_col)
        c_got[k, c] = c_all[k]

    def inner_done(k):
        drain(c_got.at[k, pl.ds(0, COLS - 1)], ar_sem.at[k, 2])
        total = jnp.concatenate([c_got[k, n] for n in range(BW)], axis=0)
        lane = lax.broadcasted_iota(jnp.int32, (BW, DEPTH), 1)
        return jnp.where(lane < IMAGE, total, 0.0), total[:, IMAGE : IMAGE + BW]

    def gram_of(first, square):
        both = 2.0 * first - dot(first, gram[...])
        rest = first - dot(both, gram[...])
        return square - dot_t(first, both) - dot_t(both, rest), rest

    def gram_cols():
        def to_col(n):
            n16 = lax.rem(c + n, COLS)
            push(m_part.at[n16], m_col.at[c], m_send.at[0], m_sem.at[0], at(r, n16))

        loop(1, COLS, to_col)

    def gram_y():
        drain(m_col.at[pl.ds(0, COLS - 1)], m_sem.at[0])
        m_one[...] = jnp.sum(m_col[...], axis=0)

        def to_y(n):
            push(m_one, m_y.at[y], m_send.at[1], m_sem.at[1], at(lax.rem(y + n, YS) * XS + x, c))

        loop(1, YS, to_y)
        m_y[y] = m_one[...]

    def gram_x():
        drain(m_y.at[pl.ds(0, YS - 1)], m_sem.at[1])
        m_two[...] = jnp.sum(m_y[...], axis=0)

        def to_x(n):
            push(m_two, m_x.at[x], m_send.at[2], m_sem.at[2], at(y * XS + lax.rem(x + n, XS), c))

        loop(1, XS, to_x)
        m_x[x] = m_two[...]

    def gram_spread():
        drain(m_x.at[pl.ds(0, XS - 1)], m_sem.at[2])
        m_all[...] = jnp.sum(m_x[...], axis=0) * inv_total

        def to_col(n):
            push(m_all, m_got.at[c], m_send.at[3], m_sem.at[3], at(r, lax.rem(c + n, COLS)))

        loop(1, COLS, to_col)
        m_got[c] = m_all[...]

    def gram_build():
        drain(m_got.at[pl.ds(0, COLS - 1)], m_sem.at[3])
        top = m_got[:, 0].reshape(128, 128)
        side = m_got[:, 1].reshape(128, 128)
        under = m_got[:, 2].reshape(128, 128)
        gram[0:128, 0:128] = top
        gram[0:128, 128:256] = side
        gram[128:256, 0:128] = side.T
        gram[128:256, 128:256] = under
        gram[256:DEPTH, :] = jnp.zeros((128, DEPTH), F32)
        for n in range(COLS):
            for j in range(3):
                gram[256 + n : 257 + n, LANES * j : LANES * (j + 1)] = m_got[n, 3, j : j + 1, :]
        gram[0:128, 256:DEPTH] = gram[256:DEPTH, 0:128].T
        gram[128:256, 256:DEPTH] = gram[256:DEPTH, 128:256].T
        clean[...] = 2.0 * stack[...] - dot(gram[...], stack[...])

    def gram_grow(inverse, rest, fresh):
        border = dot(inverse, rest)
        lane = lax.broadcasted_iota(jnp.int32, (BW, LANES), 1)
        row = lax.broadcasted_iota(jnp.int32, (BW, LANES), 0)
        gram[FRESH : FRESH + BW, 0:256] = border[:, 0:256]
        corner = jnp.where(lane < BW, border[:, 256:DEPTH], 0.0)
        block = jnp.concatenate([jnp.zeros((BW, LANES), F32), corner, jnp.zeros((96, LANES), F32)], axis=0)
        gram[256:DEPTH, 256:DEPTH] = gram[256:DEPTH, 256:DEPTH] + block + block.T
        gram[FRESH : FRESH + BW, 256:DEPTH] = corner + (lane == row + BW).astype(F32)
        gram[0:128, 256:DEPTH] = gram[256:DEPTH, 0:128].T
        gram[128:256, 256:DEPTH] = gram[256:DEPTH, 128:256].T
        clean[...] = 2.0 * stack[...] - dot(gram[...], stack[...])

    send_vectors(0)
    gram_cols()
    products(0, None)
    gram_y()
    w = image(0, last)
    inner_send(0, w)
    gram_x()
    inner_rows(0)
    gram_spread()
    inner_cols(0)
    gram_build()
    first, square = inner_done(0)
    w2 = w - dot(first, clean[...])
    sent[1] = w2.astype(BF16)
    send_vectors(1)
    square, rest = gram_of(first, square)
    lower, inverse = factor(square)
    factors_ref[0] = lower
    x1 = dot(inverse, w2)
    blocks_ref[0] = x1
    products(1, inverse)
    stack[FRESH : FRESH + BW, :] = x1
    gram_grow(inverse, rest, x1)
    w = image(1, x1)
    inner_send(1, w)
    inner_rows(1)
    inner_cols(1)
    first, square = inner_done(1)
    w2 = w - dot(first, clean[...])
    square, _ = gram_of(first, square)
    lower, inverse = factor(square)
    factors_ref[1] = lower
    blocks_ref[1] = dot(inverse, w2)

    for k in range(2):

        @pl.when(own)
        def _():
            drain(vcol.at[k, pl.ds(0, 31)], v_send.at[k])
            drain(gcol.at[k, pl.ds(0, 31)], p_send.at[k])

        @pl.when(jnp.logical_not(own))
        def _():
            drain(vcol.at[k, pl.ds(0, 32)], v_send.at[k])
            drain(gcol.at[k, pl.ds(0, 32)], p_send.at[k])

        drain(vrow.at[k, pl.ds(0, 15)], v_send.at[k])
        drain(grow.at[k, pl.ds(0, 15)], p_send.at[k])
        drain(c_col.at[k, pl.ds(0, 15)], ar_send.at[k, 0])
        drain(c_row.at[k, pl.ds(0, 31)], ar_send.at[k, 1])
        drain(c_got.at[k, pl.ds(0, 15)], ar_send.at[k, 2])
    drain(m_col.at[pl.ds(0, 15)], m_send.at[0])
    drain(m_y.at[pl.ds(0, 7)], m_send.at[1])
    drain(m_x.at[pl.ds(0, 3)], m_send.at[2])
    drain(m_got.at[pl.ds(0, 15)], m_send.at[3])


def local(tiles, tile_rows, tile_cols, tile_counts, diagonal, basis, start):
    any_spec = pl.BlockSpec(memory_space=pl.ANY)
    smem = pl.BlockSpec(memory_space=pltpu.SMEM)
    vmem = pl.BlockSpec(memory_space=pltpu.VMEM)
    dma = pltpu.SemaphoreType.DMA
    return pl.pallas_call(
        kernel,
        out_shape=(
            jax.ShapeDtypeStruct((2, BW, LANES), F32),
            jax.ShapeDtypeStruct((2, BW, BW), F32),
        ),
        in_specs=[any_spec, smem, smem, smem, any_spec, any_spec, any_spec],
        out_specs=(vmem, vmem),
        scratch_shapes=[
            pltpu.VMEM((DEPTH, LANES), F32),
            pltpu.VMEM((2, TILE, TILE), F32),
            pltpu.VMEM((2, 2, TILE, TILE), BF16),
            pltpu.VMEM((1, LANES), F32),
            pltpu.VMEM((2, BW, LANES), BF16),
            pltpu.VMEM((2, COLS, BW, LANES), BF16),
            pltpu.VMEM((2, 2 * COLS, BW, LANES), BF16),
            pltpu.VMEM((2, COLS, BW, LANES), BF16),
            pltpu.VMEM((2, 2 * COLS, BW, LANES), BF16),
            pltpu.VMEM((2, COLS, BW, LANES), BF16),
            pltpu.VMEM((2, ROWS, BW, LANES), BF16),
            pltpu.VMEM((2, COLS, 1, DEPTH), F32),
            pltpu.VMEM((2, COLS, 1, DEPTH), F32),
            pltpu.VMEM((2, 1, DEPTH), F32),
            pltpu.VMEM((2, ROWS, 1, DEPTH), F32),
            pltpu.VMEM((2, 1, DEPTH), F32),
            pltpu.VMEM((2, COLS, 1, DEPTH), F32),
            pltpu.VMEM((COLS, 4, 8, LANES), F32),
            pltpu.VMEM((COLS, 4, 8, LANES), F32),
            pltpu.VMEM((YS, 4, 8, LANES), F32),
            pltpu.VMEM((XS, 4, 8, LANES), F32),
            pltpu.VMEM((4, 8, LANES), F32),
            pltpu.VMEM((4, 8, LANES), F32),
            pltpu.VMEM((4, 8, LANES), F32),
            pltpu.VMEM((COLS, 4, 8, LANES), F32),
            pltpu.VMEM((DEPTH, DEPTH), F32),
            pltpu.VMEM((DEPTH, LANES), F32),
            dma((4,)),
            dma((2,)),
            dma((2,)),
            dma((2, 2)),
            dma((2,)),
            dma((2,)),
            dma((2,)),
            dma((2, 3)),
            dma((2, 3)),
            dma((4,)),
            dma((4,)),
        ],
        compiler_params=pltpu.CompilerParams(
            collective_id=0, has_side_effects=True, vmem_limit_bytes=48 * 1024 * 1024
        ),
    )(
        tiles.reshape(2, TILE, TILE),
        tile_rows.reshape(2),
        tile_cols.reshape(2),
        tile_counts.reshape(1),
        diagonal.reshape(1, LANES),
        basis.reshape(256, LANES),
        start,
    )


def solution(mesh):
    placed = (
        P("row", "col", None, None, None),
        P("row", "col", None),
        P("row", "col", None),
        P("row", "col"),
        P(("row", "col")),
        P(None, None, ("row", "col")),
        P(None, ("row", "col")),
    )
    return jax.shard_map(
        local,
        mesh=mesh,
        in_specs=placed,
        out_specs=(P(None, None, ("row", "col")), P()),
        check_vma=False,
    )
```

time: 1190 us -> 106 us (0.09)
  blocking collectives: 618 us -> 0 us
  waiting for transfers between devices: 525 us -> 0 us
  Pallas kernels: 0 us -> 101 us
  other arithmetic: 13.6 us -> 0 us
  between operations: 14.7 us -> 1.34 us
  matrix products: 12.8 us -> 0 us
    psum x6 -> x0, blocking collectives: 576 us -> none  [the longest x2 198 us: local(): lax.psum(project(stack_all, image_block, inv_total), ('row', 'col'))]
    psum x4 -> x0, waiting for transfers between devices: 525 us -> none  [the longest x2 293 us: local(): lax.psum(col_part.astype(jnp.bfloat16), 'row').astype(jnp.float32)]
    pallas_call x0 -> x1, Pallas kernels: none -> 101 us  [local(): pl.pallas_call(kernel, out_shape=(jax.ShapeDtypeStruct((2, BW, LANES), F3...]
    all_gather x2 -> x0, blocking collectives: 42.4 us -> none  [local(): gathered = lax.all_gather(current, 'col', axis=1, tiled=True)]
    dot_general x18 -> x0, matrix products: 12.4 us -> none  [the longest x4 5.74 us: project(): jnp.einsum('mkn,ln->mkl', stack_all, field, precision=PRECISE) * inv_total]
  transfers between devices with their start and end apart: 4 -> 0, of which waited for: 4 -> 0; matrix products, arithmetic and copies ran while one was open for 0% -> 0% of each run, Pallas kernels for 0% -> 0%
where the time goes in v1:
time: 106 us
  Pallas kernels  101 us (95%)
  local copies, waits for them, and re-layouts  3.81 us (4%)
  between operations  1.34 us (1%)
    pallas_call x1, Pallas kernels, local(): pl.pallas_call(kernel, out_shape=(jax.ShapeDtypeStruct((2, BW, LANES), F3...  101 us
    unnamed x14, local copies, waits for them, and re-layouts  3.81 us

profile of v1, /device:TPU:1, one launch (start us, length us, event | category | flops | bytes accessed | tf_op | source)
XLA Modules:
  0.0 106.1 jit_solution(3775602026658849515)
XLA Ops:
  0.6 0.0 copy-start.2
  1.3 0.0 copy-start.3
  1.3 0.0 copy-start.4
  1.3 0.0 copy-start.5
  1.3 0.0 copy-done.2
  1.3 0.6 copy-done.3
  2.0 0.0 copy-done.4
  2.0 0.0 copy-done.5
  2.0 0.0 copy-start
  2.0 1.0 copy-done
  3.0 0.0 copy-start.1
  3.0 0.9 copy-done.1
  3.9 101.0 %shard_map.86 = (f32[2,16,128]{2,1,0:T(8,128)S(1)}, f32[2,16,16]{2,1,0:T(8,128)S(1)}) custom-call(f32[2,256,256]{2,1,0:T(8,128)S(1)} %bitcast.7, s32[2]{0:T(128)S(1)} %bitcast.9, s32[2]{0:T(128)S(1)} %bitcast.10, s32[1]{0:T(128)} %bitcast.6.count_ref, f32[1,128]{1,0:T(1,128)S(1)} %bitcast.11, f32[256,128]{1,0:T(8,128)S(1)} %bitcast.8, f32[16,128]{1,0:T(8,128)S(1)} %copy-done.2), custom_call_target="tpu_custom_call" | custom-call | tf_op jit(solution)/shard_map/pallas_call | solution.py:414
  104.9 0.6 copy.12
  105.5 0.6 copy.13
Async XLA Ops:
  0.6 0.7 copy-start.2
  1.3 0.7 copy-start.3
  1.3 0.7 copy-start.4
  1.3 0.7 copy-start.5
  2.0 1.0 copy-start
  3.0 0.9 copy-start.1

commit v2 on v1

--- a/solution.py
+++ b/solution.py
@@ -43,6 +43,10 @@
         return carry
 
     lax.fori_loop(low, high, run, 0)
+
+
+def far(n, size):
+    return size // 2 + (2 * lax.rem(n, 2) - 1) * lax.div(n + 1, 2)
 
 
 def factor(gram):
@@ -70,19 +74,26 @@
     blocks_ref, factors_ref,
     stack, plates, split, dg, sent, vrow, vcol, prow, pcol, grow, gcol,
     c_part, c_col, c_sum, c_row, c_all, c_got,
-    m_part, m_col, m_y, m_x, m_one, m_two, m_all, m_got, gram, clean,
+    m_part, m_twin, m_half, m_col, m_y, m_x, m_one, m_two, m_all, m_got, gram, clean, fold,
     load_sem, v_send, vrow_sem, vcol_sem, p_send, grow_sem, gcol_sem, ar_send, ar_sem, m_send, m_sem,
 ):
     r, c = lax.axis_index("row"), lax.axis_index("col")
     y, x = r // XS, lax.rem(r, XS)
+    z, core = c // 2, lax.rem(c, 2)
     twin = lax.rem(r, COLS)
     own = c == twin
     inv_total = 1.0 / (ROWS * COLS * LANES)
 
+    def row_at(n):
+        return lax.rem(y + far(lax.div(n, XS), YS), YS) * XS + lax.rem(x + far(lax.rem(n, XS), XS), XS)
+
+    def col_at(n):
+        return lax.rem(c + far(n, COLS), COLS)
+
     loads = [
         pltpu.make_async_copy(basis_ref, stack.at[pl.ds(0, 256)], load_sem.at[0]),
         pltpu.make_async_copy(start_ref, stack.at[pl.ds(256, BW)], load_sem.at[1]),
-        pltpu.make_async_copy(tiles_ref, plates, load_sem.at[2]),
+        pltpu.make_async_copy(tiles_ref.at[0, 0], plates, load_sem.at[2]),
         pltpu.make_async_copy(diag_ref, dg, load_sem.at[3]),
     ]
     for each in loads:
@@ -112,15 +123,14 @@
     loads[1].wait()
     low, mid, last = stack[0:128, :], stack[128:256, :], stack[256:DEPTH, :][:BW]
     sent[0] = last.astype(BF16)
-    m_part[:, 0] = dot_t(low, low).reshape(COLS, 8, LANES)
-    m_part[:, 1] = dot_t(low, mid).reshape(COLS, 8, LANES)
-    m_part[:, 2] = dot_t(mid, mid).reshape(COLS, 8, LANES)
+    m_part[:, :, 0] = dot_t(low, low).reshape(2, 8, 8, LANES)
+    m_part[:, :, 1] = dot_t(low, mid).reshape(2, 8, 8, LANES)
+    m_part[:, :, 2] = dot_t(mid, mid).reshape(2, 8, 8, LANES)
     edge = dot_t(last, stack[...])
-    m_part[:, 3] = jnp.zeros((COLS, 8, LANES), F32)
+    m_part[:, :, 3] = jnp.zeros((2, 8, 8, LANES), F32)
     for k in range(COLS):
         for j in range(3):
-            m_part[k, 3, j : j + 1, :] = edge[k : k + 1, LANES * j : LANES * (j + 1)]
-    m_col[c] = m_part[c]
+            m_part[k // 8, k % 8, 3, j : j + 1, :] = edge[k : k + 1, LANES * j : LANES * (j + 1)]
     loads[2].wait()
     loads[3].wait()
     for s in range(2):
@@ -131,11 +141,11 @@
 
     weights = []
     for s in range(2):
-        row_block = r * 8 + rows_ref[s]
-        half = cols_ref[s] // 8
-        col_block = (c + COLS * half) * 8 + (cols_ref[s] - 8 * half)
+        row_block = r * 8 + rows_ref[0, 0, s]
+        half = cols_ref[0, 0, s] // 8
+        col_block = (c + COLS * half) * 8 + (cols_ref[0, 0, s] - 8 * half)
         live = jnp.where(row_block == col_block, 0.5, 1.0)
-        weights.append(jnp.where(s < count_ref[0], live, 0.0).astype(F32))
+        weights.append(jnp.where(s < count_ref[0, 0], live, 0.0).astype(F32))
 
     pl.semaphore_wait(barrier, 15 + 31 + 64)
 
@@ -144,10 +154,10 @@
         slot = COLS * (r // COLS) + c
 
         def to_twin(n):
-            target = lax.rem(r + n, ROWS)
+            target = row_at(n)
             push(src, vcol.at[k, slot], v_send.at[k], vcol_sem.at[k, r // COLS], at(target, twin))
 
-        loop(1, ROWS, to_twin)
+        loop(0, ROWS - 1, to_twin)
 
         @pl.when(own)
         def _():
@@ -155,12 +165,12 @@
 
         @pl.when(jnp.logical_not(own))
         def _():
-            to_twin(0)
+            to_twin(ROWS - 1)
 
         def to_col(n):
-            push(src, vrow.at[k, c], v_send.at[k], vrow_sem.at[k], at(r, lax.rem(c + n, COLS)))
-
-        loop(1, COLS, to_col)
+            push(src, vrow.at[k, c], v_send.at[k], vrow_sem.at[k], at(r, col_at(n)))
+
+        loop(0, COLS - 1, to_col)
         vrow[k, c] = sent[k]
 
     def drain_sized(ref, k, full, cond, sem):
@@ -172,35 +182,33 @@
         def _():
             drain(ref.at[k, pl.ds(0, full)], sem)
 
-    def products(k, inverse):
+    def products(k):
         drain(vrow.at[k, pl.ds(0, COLS - 1)], vrow_sem.at[k])
         terms = []
         for s in range(2):
-            b = 2 * rows_ref[s]
+            b = 2 * rows_ref[0, 0, s]
             vec = jnp.concatenate([vrow[k, b], vrow[k, b + 1]], axis=1)
             term = dot(vec, split[s, 0], None) + dot(vec, split[s, 1], None)
-            terms.append(term if inverse is None else dot(inverse, term))
+            terms.append(term)
         for b in range(2 * 8):
-            part = sum(terms[s] * jnp.where(cols_ref[s] == b, weights[s], 0.0) for s in range(2)).astype(BF16)
-            pcol[k, 2 * b] = part[:, :LANES]
-            pcol[k, 2 * b + 1] = part[:, LANES:]
+            part = sum(terms[s] * jnp.where(cols_ref[0, 0, s] == b, weights[s], 0.0) for s in range(2)).astype(BF16)
+            pcol[k, 2 * (b % 8), b // 8] = part[:, :LANES]
+            pcol[k, 2 * (b % 8) + 1, b // 8] = part[:, LANES:]
 
         def to_col_owner(n):
-            n16 = lax.rem(c + n, COLS)
+            target = col_at(n)
             for h in range(2):
-                push(pcol.at[k, COLS * h + n16], gcol.at[k, r], p_send.at[k], gcol_sem.at[k], at(c + COLS * h, n16))
-
-        loop(1, COLS, to_col_owner)
+
+                @pl.when(jnp.logical_or(target != c, r != c + COLS * h))
+                def _():
+                    push(pcol.at[k, target, h], gcol.at[k, r], p_send.at[k], gcol_sem.at[k], at(c + COLS * h, target))
+
+        loop(0, COLS, to_col_owner)
         for h in range(2):
-            mine = r == c + COLS * h
-
-            @pl.when(mine)
+
+            @pl.when(r == c + COLS * h)
             def _():
-                gcol[k, r] = pcol[k, COLS * h + c]
-
-            @pl.when(jnp.logical_not(mine))
-            def _():
-                push(pcol.at[k, COLS * h + c], gcol.at[k, r], p_send.at[k], gcol_sem.at[k], at(c + COLS * h, c))
+                gcol[k, r] = pcol[k, c, h]
 
         for h in range(2):
 
@@ -214,20 +222,20 @@
 
         terms = []
         for s in range(2):
-            b = 2 * cols_ref[s]
+            b = 2 * cols_ref[0, 0, s]
             vec = jnp.concatenate([vcol[k, b], vcol[k, b + 1]], axis=1)
             term = dot_t(vec, split[s, 0], None) + dot_t(vec, split[s, 1], None)
-            terms.append(term if inverse is None else dot(inverse, term))
+            terms.append(term)
         for b in range(8):
-            part = sum(terms[s] * jnp.where(rows_ref[s] == b, weights[s], 0.0) for s in range(2)).astype(BF16)
+            part = sum(terms[s] * jnp.where(rows_ref[0, 0, s] == b, weights[s], 0.0) for s in range(2)).astype(BF16)
             prow[k, 2 * b] = part[:, :LANES]
             prow[k, 2 * b + 1] = part[:, LANES:]
 
         def to_row_owner(n):
-            n16 = lax.rem(c + n, COLS)
+            n16 = col_at(n)
             push(prow.at[k, n16], grow.at[k, c], p_send.at[k], grow_sem.at[k], at(r, n16))
 
-        loop(1, COLS, to_row_owner)
+        loop(0, COLS - 1, to_row_owner)
         grow[k, c] = prow[k, c]
 
     def image(k, current):
@@ -245,10 +253,10 @@
             c_part[k, n] = partial[n : n + 1, :]
 
         def to_col(n):
-            n16 = lax.rem(c + n, COLS)
+            n16 = col_at(n)
             push(c_part.at[k, n16], c_col.at[k, c], ar_send.at[k, 0], ar_sem.at[k, 0], at(r, n16))
 
-        loop(1, COLS, to_col)
+        loop(0, COLS - 1, to_col)
         c_col[k, c] = c_part[k, c]
 
     def inner_rows(k):
@@ -256,9 +264,9 @@
         c_sum[k] = jnp.sum(c_col[k], axis=0)
 
         def to_row(n):
-            push(c_sum.at[k], c_row.at[k, r], ar_send.at[k, 1], ar_sem.at[k, 1], at(lax.rem(r + n, ROWS), c))
-
-        loop(1, ROWS, to_row)
+            push(c_sum.at[k], c_row.at[k, r], ar_send.at[k, 1], ar_sem.at[k, 1], at(row_at(n), c))
+
+        loop(0, ROWS - 1, to_row)
         c_row[k, r] = c_sum[k]
 
     def inner_cols(k):
@@ -266,9 +274,9 @@
         c_all[k] = jnp.sum(c_row[k], axis=0) * inv_total
 
         def to_col(n):
-            push(c_all.at[k], c_got.at[k, c], ar_send.at[k, 2], ar_sem.at[k, 2], at(r, lax.rem(c + n, COLS)))
-
-        loop(1, COLS, to_col)
+            push(c_all.at[k], c_got.at[k, c], ar_send.at[k, 2], ar_sem.at[k, 2], at(r, col_at(n)))
+
+        loop(0, COLS - 1, to_col)
         c_got[k, c] = c_all[k]
 
     def inner_done(k):
@@ -282,15 +290,22 @@
         rest = first - dot(both, gram[...])
         return square - dot_t(first, both) - dot_t(both, rest), rest
 
-    def gram_cols():
-        def to_col(n):
-            n16 = lax.rem(c + n, COLS)
-            push(m_part.at[n16], m_col.at[c], m_send.at[0], m_sem.at[0], at(r, n16))
-
-        loop(1, COLS, to_col)
+    def gram_pair():
+        push(m_part.at[1 - core], m_twin, m_send.at[4], m_sem.at[4], at(r, c + 1 - 2 * core))
+
+    def gram_z():
+        drain(m_twin, m_sem.at[4])
+        m_half[...] = m_part[core] + m_twin[...]
+
+        def to_z(n):
+            target = lax.rem(z + far(n, YS), YS)
+            push(m_half.at[target], m_col.at[z], m_send.at[0], m_sem.at[0], at(r, 2 * target + core))
+
+        loop(0, YS - 1, to_z)
+        m_col[z] = m_half[z]
 
     def gram_y():
-        drain(m_col.at[pl.ds(0, COLS - 1)], m_sem.at[0])
+        drain(m_col.at[pl.ds(0, YS - 1)], m_sem.at[0])
         m_one[...] = jnp.sum(m_col[...], axis=0)
 
         def to_y(n):
@@ -313,17 +328,22 @@
         drain(m_x.at[pl.ds(0, XS - 1)], m_sem.at[2])
         m_all[...] = jnp.sum(m_x[...], axis=0) * inv_total
 
-        def to_col(n):
-            push(m_all, m_got.at[c], m_send.at[3], m_sem.at[3], at(r, lax.rem(c + n, COLS)))
-
-        loop(1, COLS, to_col)
-        m_got[c] = m_all[...]
+        def to_z(n):
+            target = lax.rem(z + far(n, YS), YS)
+            push(m_all, m_got.at[core, z], m_send.at[3], m_sem.at[3], at(r, 2 * target + core))
+
+        loop(0, YS - 1, to_z)
+        m_got[core, z] = m_all[...]
+
+    def gram_share():
+        drain(m_col.at[pl.ds(0, YS - 1)], m_sem.at[3])
+        push(m_got.at[core], m_got.at[core], m_send.at[5], m_sem.at[5], at(r, c + 1 - 2 * core))
 
     def gram_build():
-        drain(m_got.at[pl.ds(0, COLS - 1)], m_sem.at[3])
-        top = m_got[:, 0].reshape(128, 128)
-        side = m_got[:, 1].reshape(128, 128)
-        under = m_got[:, 2].reshape(128, 128)
+        drain(m_twin, m_sem.at[5])
+        top = m_got[:, :, 0].reshape(128, 128)
+        side = m_got[:, :, 1].reshape(128, 128)
+        under = m_got[:, :, 2].reshape(128, 128)
         gram[0:128, 0:128] = top
         gram[0:128, 128:256] = side
         gram[128:256, 0:128] = side.T
@@ -331,7 +351,7 @@
         gram[256:DEPTH, :] = jnp.zeros((128, DEPTH), F32)
         for n in range(COLS):
             for j in range(3):
-                gram[256 + n : 257 + n, LANES * j : LANES * (j + 1)] = m_got[n, 3, j : j + 1, :]
+                gram[256 + n : 257 + n, LANES * j : LANES * (j + 1)] = m_got[n // 8, n % 8, 3, j : j + 1, :]
         gram[0:128, 256:DEPTH] = gram[256:DEPTH, 0:128].T
         gram[128:256, 256:DEPTH] = gram[256:DEPTH, 128:256].T
         clean[...] = 2.0 * stack[...] - dot(gram[...], stack[...])
@@ -349,9 +369,18 @@
         gram[128:256, 256:DEPTH] = gram[256:DEPTH, 128:256].T
         clean[...] = 2.0 * stack[...] - dot(gram[...], stack[...])
 
+    def gram_fold():
+        row = lax.broadcasted_iota(jnp.int32, (DEPTH, DEPTH), 0)
+        lane = lax.broadcasted_iota(jnp.int32, (DEPTH, DEPTH), 1)
+        eye = (row == lane).astype(F32)
+        off = eye - gram[...]
+        fold[...] = eye + off
+        fold[...] += dot(fold[...], dot(off, off))
+
+    gram_pair()
     send_vectors(0)
-    gram_cols()
-    products(0, None)
+    gram_z()
+    products(0)
     gram_y()
     w = image(0, last)
     inner_send(0, w)
@@ -359,6 +388,7 @@
     inner_rows(0)
     gram_spread()
     inner_cols(0)
+    gram_share()
     gram_build()
     first, square = inner_done(0)
     w2 = w - dot(first, clean[...])
@@ -369,16 +399,17 @@
     factors_ref[0] = lower
     x1 = dot(inverse, w2)
     blocks_ref[0] = x1
-    products(1, inverse)
+    products(1)
     stack[FRESH : FRESH + BW, :] = x1
     gram_grow(inverse, rest, x1)
-    w = image(1, x1)
+    gram_fold()
+    w = dot(inverse, image(1, w2))
     inner_send(1, w)
     inner_rows(1)
     inner_cols(1)
     first, square = inner_done(1)
     w2 = w - dot(first, clean[...])
-    square, _ = gram_of(first, square)
+    square -= dot_t(first, dot(first, fold[...]))
     lower, inverse = factor(square)
     factors_ref[1] = lower
     blocks_ref[1] = dot(inverse, w2)
@@ -400,14 +431,16 @@
         drain(c_col.at[k, pl.ds(0, 15)], ar_send.at[k, 0])
         drain(c_row.at[k, pl.ds(0, 31)], ar_send.at[k, 1])
         drain(c_got.at[k, pl.ds(0, 15)], ar_send.at[k, 2])
-    drain(m_col.at[pl.ds(0, 15)], m_send.at[0])
+    drain(m_col.at[pl.ds(0, 7)], m_send.at[0])
     drain(m_y.at[pl.ds(0, 7)], m_send.at[1])
     drain(m_x.at[pl.ds(0, 3)], m_send.at[2])
-    drain(m_got.at[pl.ds(0, 15)], m_send.at[3])
+    drain(m_col.at[pl.ds(0, 7)], m_send.at[3])
+    drain(m_twin, m_send.at[4])
+    drain(m_twin, m_send.at[5])
 
 
 def local(tiles, tile_rows, tile_cols, tile_counts, diagonal, basis, start):
-    any_spec = pl.BlockSpec(memory_space=pl.ANY)
+    any_spec = pl.BlockSpec(memory_space=pltpu.HBM)
     smem = pl.BlockSpec(memory_space=pltpu.SMEM)
     vmem = pl.BlockSpec(memory_space=pltpu.VMEM)
     dma = pltpu.SemaphoreType.DMA
@@ -428,7 +461,7 @@
             pltpu.VMEM((2, COLS, BW, LANES), BF16),
             pltpu.VMEM((2, 2 * COLS, BW, LANES), BF16),
             pltpu.VMEM((2, COLS, BW, LANES), BF16),
-            pltpu.VMEM((2, 2 * COLS, BW, LANES), BF16),
+            pltpu.VMEM((2, COLS, 2, BW, LANES), BF16),
             pltpu.VMEM((2, COLS, BW, LANES), BF16),
             pltpu.VMEM((2, ROWS, BW, LANES), BF16),
             pltpu.VMEM((2, COLS, 1, DEPTH), F32),
@@ -437,16 +470,19 @@
             pltpu.VMEM((2, ROWS, 1, DEPTH), F32),
             pltpu.VMEM((2, 1, DEPTH), F32),
             pltpu.VMEM((2, COLS, 1, DEPTH), F32),
-            pltpu.VMEM((COLS, 4, 8, LANES), F32),
-            pltpu.VMEM((COLS, 4, 8, LANES), F32),
+            pltpu.VMEM((2, 8, 4, 8, LANES), F32),
+            pltpu.VMEM((8, 4, 8, LANES), F32),
+            pltpu.VMEM((8, 4, 8, LANES), F32),
+            pltpu.VMEM((8, 4, 8, LANES), F32),
             pltpu.VMEM((YS, 4, 8, LANES), F32),
             pltpu.VMEM((XS, 4, 8, LANES), F32),
             pltpu.VMEM((4, 8, LANES), F32),
             pltpu.VMEM((4, 8, LANES), F32),
             pltpu.VMEM((4, 8, LANES), F32),
-            pltpu.VMEM((COLS, 4, 8, LANES), F32),
+            pltpu.VMEM((2, 8, 4, 8, LANES), F32),
             pltpu.VMEM((DEPTH, DEPTH), F32),
             pltpu.VMEM((DEPTH, LANES), F32),
+            pltpu.VMEM((DEPTH, DEPTH), F32),
             dma((4,)),
             dma((2,)),
             dma((2,)),
@@ -456,17 +492,17 @@
             dma((2,)),
             dma((2, 3)),
             dma((2, 3)),
-            dma((4,)),
-            dma((4,)),
+            dma((6,)),
+            dma((6,)),
         ],
         compiler_params=pltpu.CompilerParams(
-            collective_id=0, has_side_effects=True, vmem_limit_bytes=48 * 1024 * 1024
+            collective_id=0, has_side_effects=True, vmem_limit_bytes=60 * 1024 * 1024
         ),
     )(
-        tiles.reshape(2, TILE, TILE),
-        tile_rows.reshape(2),
-        tile_cols.reshape(2),
-        tile_counts.reshape(1),
+        tiles,
+        tile_rows,
+        tile_cols,
+        tile_counts,
         diagonal.reshape(1, LANES),
         basis.reshape(256, LANES),
         start,

time: 106 us -> 102 us (0.962)
  Pallas kernels: 101 us -> 99 us
  local copies, waits for them, and re-layouts: 3.81 us -> 1.94 us
    pallas_call x1, Pallas kernels: 101 us -> 99 us  [local(): pl.pallas_call(kernel, out_shape=(jax.ShapeDtypeStruct((2, BW, LANES), F3...]
    unnamed x14 -> x4, local copies, waits for them, and re-layouts: 3.81 us -> 1.94 us
where the time goes in v2:
time: 102 us
  Pallas kernels  99 us (97%)
  local copies, waits for them, and re-layouts  1.94 us (2%)
  between operations  1.29 us (1%)
    pallas_call x1, Pallas kernels, local(): pl.pallas_call(kernel, out_shape=(jax.ShapeDtypeStruct((2, BW, LANES), F3...  99 us

profile of v2, /device:TPU:1, one launch (start us, length us, event | category | flops | bytes accessed | tf_op | source)
XLA Modules:
  0.0 102.2 jit_solution(685500024754704913)
XLA Ops:
  1.3 99.0 %shard_map.86 = (f32[2,16,128]{2,1,0:T(8,128)}, f32[2,16,16]{2,1,0:T(8,128)}) custom-call(f32[1,1,2,256,256]{4,3,2,1,0:T(8,128)} %tiles_ref.1, s32[1,1,2]{2,1,0:T(1,128)} %rows_ref.1, s32[1,1,2]{2,1,0:T(1,128)} %cols_ref.1, s32[1,1]{1,0:T(1,128)S(6)} %copy.11.count_ref, f32[1,128]{1,0:T(1,128)} %bitcast.3, f32[256,128]{1,0:T(8,128)} %bitcast.2, ...), custom_call_target="tpu_custom_call" | custom-call | tf_op jit(solution)/shard_map/pallas_call | solution.py:447
  100.3 0.0 copy-start
  100.3 1.3 %copy.12 = f32[2,16,128]{2,1,0:T(8,128)} copy(f32[2,16,128]{2,1,0:T(8,128)} %get-tuple-element.4) | data formatting | bytes 32768
  101.6 0.0 copy-done
  101.6 0.6 copy.13
Async XLA Ops:
  100.3 1.3 %copy-start = (f32[2,16,16]{2,1,0:T(8,128)S(1)}, f32[2,16,16]{2,1,0:T(8,128)}, u32[]{:S(2)}) copy-start(f32[2,16,16]{2,1,0:T(8,128)} %get-tuple-element.5) | copy-start | bytes 6148

commit v3 on v2

--- a/solution.py
+++ b/solution.py
@@ -74,7 +74,7 @@
     blocks_ref, factors_ref,
     stack, plates, split, dg, sent, vrow, vcol, prow, pcol, grow, gcol,
     c_part, c_col, c_sum, c_row, c_all, c_got,
-    m_part, m_twin, m_half, m_col, m_y, m_x, m_one, m_two, m_all, m_got, gram, clean, fold,
+    m_part, m_twin, m_half, m_x, m_one, m_y, m_two, m_z, m_all, m_back, m_got, gram, clean, fold,
     load_sem, v_send, vrow_sem, vcol_sem, p_send, grow_sem, gcol_sem, ar_send, ar_sem, m_send, m_sem,
 ):
     r, c = lax.axis_index("row"), lax.axis_index("col")
@@ -105,32 +105,32 @@
         pl.semaphore_signal(barrier, inc=1, device_id=target, device_id_type=MESH)
 
     def greet_rows(k):
-        greet(at(lax.rem(r + k, ROWS), c))
+        greet(at(row_at(k), c))
 
     def greet_cols(k):
-        greet(at(r, lax.rem(c + k, COLS)))
+        greet(at(r, col_at(k)))
 
     def greet_twins(k):
-        greet(at(lax.rem(r + k, ROWS), twin))
-        greet(at(c + COLS * (k // COLS), lax.rem(k, COLS)))
+        greet(at(row_at(k), twin))
+        greet(at(c + COLS * lax.rem(k, 2), col_at(lax.div(k, 2))))
 
     loop(0, ROWS, greet_twins)
-    loop(1, ROWS, greet_rows)
-    loop(1, COLS, greet_cols)
+    loop(0, ROWS - 1, greet_rows)
+    loop(0, COLS - 1, greet_cols)
 
     stack[FRESH:DEPTH, :] = jnp.zeros((DEPTH - FRESH, LANES), F32)
     loads[0].wait()
     loads[1].wait()
     low, mid, last = stack[0:128, :], stack[128:256, :], stack[256:DEPTH, :][:BW]
     sent[0] = last.astype(BF16)
-    m_part[:, :, 0] = dot_t(low, low).reshape(2, 8, 8, LANES)
-    m_part[:, :, 1] = dot_t(low, mid).reshape(2, 8, 8, LANES)
-    m_part[:, :, 2] = dot_t(mid, mid).reshape(2, 8, 8, LANES)
+    m_part[:, :, :, 0] = dot_t(low, low).reshape(2, 4, 2, 8, LANES)
+    m_part[:, :, :, 1] = dot_t(low, mid).reshape(2, 4, 2, 8, LANES)
+    m_part[:, :, :, 2] = dot_t(mid, mid).reshape(2, 4, 2, 8, LANES)
     edge = dot_t(last, stack[...])
-    m_part[:, :, 3] = jnp.zeros((2, 8, 8, LANES), F32)
+    m_part[:, :, :, 3] = jnp.zeros((2, 4, 2, 8, LANES), F32)
     for k in range(COLS):
         for j in range(3):
-            m_part[k // 8, k % 8, 3, j : j + 1, :] = edge[k : k + 1, LANES * j : LANES * (j + 1)]
+            m_part[k // 8, k % 8 // 2, k % 2, 3, j : j + 1, :] = edge[k : k + 1, LANES * j : LANES * (j + 1)]
     loads[2].wait()
     loads[3].wait()
     for s in range(2):
@@ -293,57 +293,71 @@
     def gram_pair():
         push(m_part.at[1 - core], m_twin, m_send.at[4], m_sem.at[4], at(r, c + 1 - 2 * core))
 
-    def gram_z():
+    def gram_x():
         drain(m_twin, m_sem.at[4])
         m_half[...] = m_part[core] + m_twin[...]
 
-        def to_z(n):
-            target = lax.rem(z + far(n, YS), YS)
-            push(m_half.at[target], m_col.at[z], m_send.at[0], m_sem.at[0], at(r, 2 * target + core))
-
-        loop(0, YS - 1, to_z)
-        m_col[z] = m_half[z]
+        def to_x(n):
+            target = lax.rem(x + far(n, XS), XS)
+            push(m_half.at[target], m_x.at[x], m_send.at[0], m_sem.at[0], at(y * XS + target, c))
+
+        loop(0, XS - 1, to_x)
+        m_x[x] = m_half[x]
 
     def gram_y():
-        drain(m_col.at[pl.ds(0, YS - 1)], m_sem.at[0])
-        m_one[...] = jnp.sum(m_col[...], axis=0)
+        drain(m_x.at[pl.ds(0, XS - 1)], m_sem.at[0])
+        m_one[...] = jnp.sum(m_x[...], axis=0)
 
         def to_y(n):
-            push(m_one, m_y.at[y], m_send.at[1], m_sem.at[1], at(lax.rem(y + n, YS) * XS + x, c))
-
-        loop(1, YS, to_y)
-        m_y[y] = m_one[...]
-
-    def gram_x():
+            target = lax.rem(y + far(n, YS), YS)
+            piece = m_one.at[lax.div(target, 4), lax.rem(target, 4)]
+            push(piece, m_y.at[y], m_send.at[1], m_sem.at[1], at(target * XS + x, c))
+
+        loop(0, YS - 1, to_y)
+        m_y[y] = m_one[lax.div(y, 4), lax.rem(y, 4)]
+
+    def gram_z():
         drain(m_y.at[pl.ds(0, YS - 1)], m_sem.at[1])
         m_two[...] = jnp.sum(m_y[...], axis=0)
 
+        def to_z(n):
+            target = lax.rem(z + far(n, 8), 8)
+            push(m_two, m_z.at[z], m_send.at[2], m_sem.at[2], at(r, 2 * target + core))
+
+        loop(0, 7, to_z)
+        m_z[z] = m_two[...]
+
+    def gram_y_back():
+        drain(m_z.at[pl.ds(0, 7)], m_sem.at[2])
+        m_all[...] = jnp.sum(m_z[...], axis=0) * inv_total
+        mine = lax.div(y, 4), lax.rem(y, 4)
+
+        def to_y(n):
+            target = lax.rem(y + far(n, YS), YS)
+            push(m_all, m_back.at[mine], m_send.at[3], m_sem.at[3], at(target * XS + x, c))
+
+        loop(0, YS - 1, to_y)
+        m_back[mine] = m_all[...]
+
+    def gram_x_back():
+        drain(m_z.at[pl.ds(0, 7)], m_sem.at[3])
+
         def to_x(n):
-            push(m_two, m_x.at[x], m_send.at[2], m_sem.at[2], at(y * XS + lax.rem(x + n, XS), c))
-
-        loop(1, XS, to_x)
-        m_x[x] = m_two[...]
-
-    def gram_spread():
-        drain(m_x.at[pl.ds(0, XS - 1)], m_sem.at[2])
-        m_all[...] = jnp.sum(m_x[...], axis=0) * inv_total
-
-        def to_z(n):
-            target = lax.rem(z + far(n, YS), YS)
-            push(m_all, m_got.at[core, z], m_send.at[3], m_sem.at[3], at(r, 2 * target + core))
-
-        loop(0, YS - 1, to_z)
-        m_got[core, z] = m_all[...]
+            target = lax.rem(x + far(n, XS), XS)
+            push(m_back, m_got.at[core, x], m_send.at[6], m_sem.at[6], at(y * XS + target, c))
+
+        loop(0, XS - 1, to_x)
+        m_got[core, x] = m_back[...]
 
     def gram_share():
-        drain(m_col.at[pl.ds(0, YS - 1)], m_sem.at[3])
+        drain(m_x.at[pl.ds(0, XS - 1)], m_sem.at[6])
         push(m_got.at[core], m_got.at[core], m_send.at[5], m_sem.at[5], at(r, c + 1 - 2 * core))
 
     def gram_build():
         drain(m_twin, m_sem.at[5])
-        top = m_got[:, :, 0].reshape(128, 128)
-        side = m_got[:, :, 1].reshape(128, 128)
-        under = m_got[:, :, 2].reshape(128, 128)
+        top = m_got[:, :, :, 0].reshape(128, 128)
+        side = m_got[:, :, :, 1].reshape(128, 128)
+        under = m_got[:, :, :, 2].reshape(128, 128)
         gram[0:128, 0:128] = top
         gram[0:128, 128:256] = side
         gram[128:256, 0:128] = side.T
@@ -351,7 +365,7 @@
         gram[256:DEPTH, :] = jnp.zeros((128, DEPTH), F32)
         for n in range(COLS):
             for j in range(3):
-                gram[256 + n : 257 + n, LANES * j : LANES * (j + 1)] = m_got[n // 8, n % 8, 3, j : j + 1, :]
+                gram[256 + n : 257 + n, LANES * j : LANES * (j + 1)] = m_got[n // 8, n % 8 // 2, n % 2, 3, j : j + 1, :]
         gram[0:128, 256:DEPTH] = gram[256:DEPTH, 0:128].T
         gram[128:256, 256:DEPTH] = gram[256:DEPTH, 128:256].T
         clean[...] = 2.0 * stack[...] - dot(gram[...], stack[...])
@@ -379,14 +393,15 @@
 
     gram_pair()
     send_vectors(0)
-    gram_z()
+    gram_x()
     products(0)
     gram_y()
+    gram_z()
     w = image(0, last)
     inner_send(0, w)
-    gram_x()
+    gram_y_back()
     inner_rows(0)
-    gram_spread()
+    gram_x_back()
     inner_cols(0)
     gram_share()
     gram_build()
@@ -431,12 +446,13 @@
         drain(c_col.at[k, pl.ds(0, 15)], ar_send.at[k, 0])
         drain(c_row.at[k, pl.ds(0, 31)], ar_send.at[k, 1])
         drain(c_got.at[k, pl.ds(0, 15)], ar_send.at[k, 2])
-    drain(m_col.at[pl.ds(0, 7)], m_send.at[0])
+    drain(m_x.at[pl.ds(0, 3)], m_send.at[0])
     drain(m_y.at[pl.ds(0, 7)], m_send.at[1])
-    drain(m_x.at[pl.ds(0, 3)], m_send.at[2])
-    drain(m_col.at[pl.ds(0, 7)], m_send.at[3])
+    drain(m_y.at[pl.ds(0, 7)], m_send.at[2])
+    drain(m_y.at[pl.ds(0, 7)], m_send.at[3])
     drain(m_twin, m_send.at[4])
     drain(m_twin, m_send.at[5])
+    drain(m_x.at[pl.ds(0, 3)], m_send.at[6])
 
 
 def local(tiles, tile_rows, tile_cols, tile_counts, diagonal, basis, start):
@@ -470,16 +486,17 @@
             pltpu.VMEM((2, ROWS, 1, DEPTH), F32),
             pltpu.VMEM((2, 1, DEPTH), F32),
             pltpu.VMEM((2, COLS, 1, DEPTH), F32),
-            pltpu.VMEM((2, 8, 4, 8, LANES), F32),
-            pltpu.VMEM((8, 4, 8, LANES), F32),
-            pltpu.VMEM((8, 4, 8, LANES), F32),
-            pltpu.VMEM((8, 4, 8, LANES), F32),
-            pltpu.VMEM((YS, 4, 8, LANES), F32),
-            pltpu.VMEM((XS, 4, 8, LANES), F32),
-            pltpu.VMEM((4, 8, LANES), F32),
-            pltpu.VMEM((4, 8, LANES), F32),
-            pltpu.VMEM((4, 8, LANES), F32),
-            pltpu.VMEM((2, 8, 4, 8, LANES), F32),
+            pltpu.VMEM((2, XS, 2, 4, 8, LANES), F32),
+            pltpu.VMEM((XS, 2, 4, 8, LANES), F32),
+            pltpu.VMEM((XS, 2, 4, 8, LANES), F32),
+            pltpu.VMEM((XS, 2, 4, 8, LANES), F32),
+            pltpu.VMEM((2, 4, 8, LANES), F32),
+            pltpu.VMEM((YS, 8, LANES), F32),
+            pltpu.VMEM((8, LANES), F32),
+            pltpu.VMEM((8, 8, LANES), F32),
+            pltpu.VMEM((8, LANES), F32),
+            pltpu.VMEM((2, 4, 8, LANES), F32),
+            pltpu.VMEM((2, XS, 2, 4, 8, LANES), F32),
             pltpu.VMEM((DEPTH, DEPTH), F32),
             pltpu.VMEM((DEPTH, LANES), F32),
             pltpu.VMEM((DEPTH, DEPTH), F32),
@@ -492,8 +509,8 @@
             dma((2,)),
             dma((2, 3)),
             dma((2, 3)),
-            dma((6,)),
-            dma((6,)),
+            dma((7,)),
+            dma((7,)),
         ],
         compiler_params=pltpu.CompilerParams(
             collective_id=0, has_side_effects=True, vmem_limit_bytes=60 * 1024 * 1024

time: 102 us -> 102 us (level)
  no operation moved by 1% of the time
where the time goes in v3:
time: 102 us
  Pallas kernels  98.3 us (96%)
  local copies, waits for them, and re-layouts  1.94 us (2%)
  between operations  1.29 us (1%)
    pallas_call x1, Pallas kernels, local(): pl.pallas_call(kernel, out_shape=(jax.ShapeDtypeStruct((2, BW, LANES), F3...  98.3 us

profile of v3, /device:TPU:1, one launch (start us, length us, event | category | flops | bytes accessed | tf_op | source)
XLA Modules:
  0.0 101.5 jit_solution(16976573584950729057)
XLA Ops:
  1.3 98.3 %shard_map.86 = (f32[2,16,128]{2,1,0:T(8,128)}, f32[2,16,16]{2,1,0:T(8,128)}) custom-call(f32[1,1,2,256,256]{4,3,2,1,0:T(8,128)} %tiles_ref.1, s32[1,1,2]{2,1,0:T(1,128)} %rows_ref.1, s32[1,1,2]{2,1,0:T(1,128)} %cols_ref.1, s32[1,1]{1,0:T(1,128)S(6)} %copy.11.count_ref, f32[1,128]{1,0:T(1,128)} %bitcast.3, f32[256,128]{1,0:T(8,128)} %bitcast.2, ...), custom_call_target="tpu_custom_call" | custom-call | tf_op jit(solution)/shard_map/pallas_call | solution.py:463
  99.6 0.0 copy-start
  99.6 1.3 %copy.12 = f32[2,16,128]{2,1,0:T(8,128)} copy(f32[2,16,128]{2,1,0:T(8,128)} %get-tuple-element.4) | data formatting | bytes 32768
  100.9 0.0 copy-done
  100.9 0.6 copy.13
Async XLA Ops:
  99.6 1.3 %copy-start = (f32[2,16,16]{2,1,0:T(8,128)S(1)}, f32[2,16,16]{2,1,0:T(8,128)}, u32[]{:S(2)}) copy-start(f32[2,16,16]{2,1,0:T(8,128)} %get-tuple-element.5) | copy-start | bytes 6148

commit v4 on v3

--- a/solution.py
+++ b/solution.py
@@ -56,15 +56,21 @@
     work = jnp.concatenate([gram, jnp.zeros((BW, LANES - BW), F32)], axis=1) + eye
     lower = jnp.zeros((BW, LANES), F32)
     scale = jnp.zeros((BW, LANES), F32)
-    for j in range(BW):
-        pivot_row = work[j : j + 1, :]
-        column = work[:, j : j + 1]
-        pivot = pivot_row[:, j : j + 1]
-        root = 1.0 / jnp.sqrt(pivot)
-        lower = jnp.where((lane == j) & (row >= j), column * root, lower)
-        scale = jnp.where(row == j, root, scale)
-        step = jnp.where(row > j, column * (1.0 / pivot), 0.0)
-        work = work - step * pivot_row
+    for j in range(0, BW, 2):
+        row_one, row_two = work[j : j + 1, :], work[j + 1 : j + 2, :]
+        col_one, col_two = work[:, j : j + 1], work[:, j + 1 : j + 2]
+        one, side, two = row_one[:, j : j + 1], row_one[:, j + 1 : j + 2], row_two[:, j + 1 : j + 2]
+        share = 1.0 / one
+        ratio = side * share
+        two = two - ratio * side
+        root_one, root_two = 1.0 / jnp.sqrt(one), 1.0 / jnp.sqrt(two)
+        row_two = row_two - ratio * row_one
+        col_two = col_two - ratio * col_one
+        lower = jnp.where((lane == j) & (row >= j), col_one * root_one, lower)
+        lower = jnp.where((lane == j + 1) & (row > j), col_two * root_two, lower)
+        scale = jnp.where(row == j, root_one, jnp.where(row == j + 1, root_two, scale))
+        step = jnp.where(row > j + 1, col_one * (share * row_one) + col_two * ((1.0 / two) * row_two), 0.0)
+        work = jnp.where(row == j + 1, row_two, work - step)
     inverse = (work * scale)[:, BW : 2 * BW]
     return lower[:, :BW], inverse
 
@@ -157,6 +163,10 @@
             target = row_at(n)
             push(src, vcol.at[k, slot], v_send.at[k], vcol_sem.at[k, r // COLS], at(target, twin))
 
+        def to_col(n):
+            push(src, vrow.at[k, c], v_send.at[k], vrow_sem.at[k], at(r, col_at(n)))
+
+        loop(0, COLS - 1, to_col)
         loop(0, ROWS - 1, to_twin)
 
         @pl.when(own)
@@ -167,10 +177,6 @@
         def _():
             to_twin(ROWS - 1)
 
-        def to_col(n):
-            push(src, vrow.at[k, c], v_send.at[k], vrow_sem.at[k], at(r, col_at(n)))
-
-        loop(0, COLS - 1, to_col)
         vrow[k, c] = sent[k]
 
     def drain_sized(ref, k, full, cond, sem):

time: 102 us -> 97.5 us (0.956)
  Pallas kernels: 98.3 us -> 94.1 us
    pallas_call x1, Pallas kernels: 98.3 us -> 94.1 us  [local(): pl.pallas_call(kernel, out_shape=(jax.ShapeDtypeStruct((2, BW, LANES), F3...]
where the time goes in v4:
time: 97.5 us; the launch traced here: 97.3 us
  Pallas kernels  94.1 us (97%)
  local copies, waits for them, and re-layouts  1.94 us (2%)
  between operations  1.29 us (1%)
    pallas_call x1, Pallas kernels, local(): pl.pallas_call(kernel, out_shape=(jax.ShapeDtypeStruct((2, BW, LANES), F3...  94.1 us

profile of v4, /device:TPU:1, one launch (start us, length us, event | category | flops | bytes accessed | tf_op | source)
XLA Modules:
  0.0 97.3 jit_solution(16164752343712899660)
XLA Ops:
  1.3 94.1 %shard_map.86 = (f32[2,16,128]{2,1,0:T(8,128)}, f32[2,16,16]{2,1,0:T(8,128)}) custom-call(f32[1,1,2,256,256]{4,3,2,1,0:T(8,128)} %tiles_ref.1, s32[1,1,2]{2,1,0:T(1,128)} %rows_ref.1, s32[1,1,2]{2,1,0:T(1,128)} %cols_ref.1, s32[1,1]{1,0:T(1,128)S(6)} %copy.11.count_ref, f32[1,128]{1,0:T(1,128)} %bitcast.3, f32[256,128]{1,0:T(8,128)} %bitcast.2, ...), custom_call_target="tpu_custom_call" | custom-call | tf_op jit(solution)/shard_map/pallas_call | solution.py:469
  95.4 0.0 copy-start
  95.4 1.3 %copy.12 = f32[2,16,128]{2,1,0:T(8,128)} copy(f32[2,16,128]{2,1,0:T(8,128)} %get-tuple-element.4) | data formatting | bytes 32768
  96.7 0.0 copy-done
  96.7 0.6 copy.13
Async XLA Ops:
  95.4 1.3 %copy-start = (f32[2,16,16]{2,1,0:T(8,128)S(1)}, f32[2,16,16]{2,1,0:T(8,128)}, u32[]{:S(2)}) copy-start(f32[2,16,16]{2,1,0:T(8,128)} %get-tuple-element.5) | copy-start | bytes 6148
